TPU v7x, 128 devices: a whole 4x4x4 slice. The times are simulated.
128 devices in a mesh: box: 32 (over x, z, core), grp: 4 (over y).
Axes of the slice: x: 4, y: 4, z: 4, core: 2. Of those that a mesh axis runs over, the one named last changes fastest.
Arguments:
- coupling: bfloat16 [512, 256, 768], P(('box', 'grp')), may hold values from -1.1953125 to 1.1953125
- inverse: bfloat16 [512, 768, 768], P(('box', 'grp')), may hold values from -0.21875 to 0.21875
- tiles: bfloat16 [512, 6, 768, 256], P(('box', 'grp')), may hold values from -1.1953125 to 1.1953125
- near_block: bfloat16 [512, 256, 1792], P(('box', 'grp')), may hold values from -3 to 3
- neighbour: int32 [512, 6], P(('box', 'grp')), may hold values from 0 to 511, as said below
- source_slot: int32 [512, 6], P(('box', 'grp')), may hold values from 0 to 5
Outputs:
- updated: bfloat16 [512, 256, 1792], P('grp', 'box')
Inputs may be any that keep to these rules, and one draw needn't show every extreme that they name: `neighbour`: the box storing a slot's tile lies on the device holding the box, or on the device just before or after it in the order of box+grp, cyclically. Every tile is read by exactly one slot of one box. Between two adjacent devices as many tiles are read in one direction as in the other, at most 12, and exactly 12 between some pair of devices.
All inputs are finite; a program needn't handle non-finite values.
Results may differ from a plain program's by a relative error of at most 0.008.
Values may be sent and summed in bfloat16 or wider, within the bound.
A program may use at most 128 MiB of HBM per device.

v0:
```python
import jax
import jax.numpy as jnp
from jax import lax
from jax.sharding import PartitionSpec as P

FAR = 12


def padded(block, sides, width):
    for axis, dim in sides:
        count = lax.axis_size(axis)
        forward = [(i, i + 1) for i in range(count - 1)]
        forward.append((count - 1, 0))
        backward = [(target, source) for source, target in forward]
        low = lax.ppermute(
            lax.slice_in_dim(block, block.shape[dim] - width, None, axis=dim), axis, forward
        )
        high = lax.ppermute(lax.slice_in_dim(block, 0, width, axis=dim), axis, backward)
        block = jnp.concatenate([low, block, high], axis=dim)
    return block


def from_behind(block, axis, distance):
    devices = range(lax.axis_size(axis))
    route = [((i - distance) % len(devices), i) for i in devices]
    return lax.ppermute(block, axis, route)


def source_index(requests, owner_first, slot_count):
    return (requests[:, 0] - owner_first) * slot_count + requests[:, 1]


def compact_rows(requests, owner_device, box_count, slot_count, capacity):
    wanted = requests[:, 0] // box_count == owner_device
    ranking = jnp.cumsum(wanted.astype(jnp.int32)) - 1
    places = jnp.arange(capacity, dtype=jnp.int32)
    onehot = jnp.logical_and(ranking[None, :] == places[:, None], wanted[None, :]).astype(jnp.int32)
    sources = jnp.clip(
        source_index(requests, owner_device * box_count, slot_count), 0, box_count * slot_count - 1
    )
    requesters = jnp.arange(requests.shape[0], dtype=jnp.int32) // slot_count
    return (
        jnp.sum(onehot * sources[None, :], axis=1),
        jnp.sum(onehot * requesters[None, :], axis=1),
    )


def arrival_index(requests, device_now, device_count, box_count, slot_count, capacity):
    source_device = requests[:, 0] // box_count
    from_after = source_device == (device_now + 1) % device_count
    from_before = source_device == (device_now + device_count - 1) % device_count
    rank_after = jnp.cumsum(from_after.astype(jnp.int32)) - 1
    rank_before = jnp.cumsum(from_before.astype(jnp.int32)) - 1
    total = box_count * slot_count
    local_rows = jnp.clip(source_index(requests, device_now * box_count, slot_count), 0, total - 1)
    index = jnp.where(
        from_after,
        total + rank_after,
        jnp.where(from_before, total + capacity + rank_before, local_rows),
    )
    return (index, jnp.logical_or(from_after, from_before), local_rows)


def per_device(coupling, inverse, tiles, near_block, neighbour, source_slot):
    box_count, skel_rows, red_rows = coupling.shape
    slot_count = neighbour.shape[1]
    capacity = FAR
    total = box_count * slot_count
    device_count = lax.axis_size(("box", "grp"))
    device_now = lax.axis_index(("box", "grp"))
    weights = jnp.einsum(
        "akr,ars->aks", coupling, inverse, preferred_element_type=jnp.float32
    ).astype(jnp.bfloat16)
    requests = jnp.stack([neighbour, source_slot], axis=2)
    beside_all = padded(requests, ((("box", "grp"), 0),), box_count)
    before_req = beside_all[:box_count].reshape(-1, 2)
    after_req = beside_all[2 * box_count :].reshape(-1, 2)
    back_src, back_who = compact_rows(before_req, device_now, box_count, slot_count, capacity)
    ahead_src, ahead_who = compact_rows(after_req, device_now, box_count, slot_count, capacity)
    index, remote, local_rows = arrival_index(
        requests.reshape(-1, 2), device_now, device_count, box_count, slot_count, capacity
    )
    tile_rows = tiles.reshape(total, red_rows, skel_rows)
    from_after = from_behind(tile_rows[back_src], ("box", "grp"), -1)
    from_before = from_behind(tile_rows[ahead_src], ("box", "grp"), 1)
    tile_pool = jnp.concatenate([tile_rows, from_after, from_before], axis=0)
    picked = tile_pool[index].reshape(box_count, slot_count, red_rows, skel_rows)
    update = jnp.einsum("akr,ajrc->akjc", weights, picked, preferred_element_type=jnp.float32)
    own_term = jnp.einsum("akr,acr->akc", weights, coupling, preferred_element_type=jnp.float32)
    combined = jnp.concatenate([own_term[:, :, None, :], update], axis=2).reshape(
        box_count, skel_rows, -1
    )
    fine_rows = (near_block.astype(jnp.float32) - combined).astype(jnp.bfloat16)
    packed = fine_rows.reshape(1, box_count, skel_rows, fine_rows.shape[-1])
    moved = lax.all_to_all(
        lax.all_to_all(packed, "box", split_axis=2, concat_axis=0, tiled=True),
        "grp",
        split_axis=0,
        concat_axis=1,
        tiled=True,
    )
    return moved.reshape(-1, skel_rows // lax.axis_size("box"), moved.shape[-1])


def solution(mesh):
    return jax.shard_map(
        per_device,
        mesh=mesh,
        in_specs=(
            P(("box", "grp"), None, None),
            P(("box", "grp"), None, None),
            P(("box", "grp"), None, None, None),
            P(("box", "grp"), None, None),
            P(("box", "grp"), None),
            P(("box", "grp"), None),
        ),
        out_specs=P("grp", "box", None),
        check_vma=False,
    )
```

profile of v0, /device:TPU:0, one launch (start us, length us, event | category | flops | bytes accessed | tf_op | source)
XLA Modules:
  0.0 286.8 jit_solution(16313634517677705274)
XLA Ops:
  0.0 0.8 pad_add_fusion
  0.8 1.7 collective-permute-start
  2.5 6.5 %collective-permute-start.2 = (s32[4,6,2]{1,0,2:T(4,128)S(1)}, s32[4,6,2]{1,0,2:T(4,128)S(1)}, u32[]{:S(2)}, u32[]{:S(2)}) collective-permute-start(s32[4,6,2]{1,0,2:T(4,128)S(1)} %pad_add_fusion), channel_id=1, source_target_pairs={{1,0},{2,1},{3,2},{4,3},{5,4},{6,5},{7,6},{8,7},{9,8},{10,9},{11,1... | collective-permute-start | bytes 584 | tf_op jit(solution)/shard_map/ppermute | solution.py:18
  9.0 1.3 collective-permute-done
  10.3 0.1 reshape.340
  10.4 0.1 reshape.341
  10.5 0.1 copy.103
  10.6 0.1 copy.104
  10.8 0.1 add_reduce_fusion.1
  10.9 0.1 select_reduce_fusion.1
  11.0 6.8 %gather_fusion = bf16[12,768,256]{2,1,0:T(8,128)(2,1)} fusion(bf16[24,768,256]{2,1,0:T(8,128)(2,1)} %bitcast.88, s32[1024]{0:T(1024)S(1)} %pad_clamp_fusion.2), kind=kCustom, calls=%fused_computation | custom fusion | bytes 9437232 | tf_op jit(solution)/shard_map/gather | solution.py:84
  17.9 7.1 %collective-permute-start.1 = (bf16[12,768,256]{2,1,0:T(8,128)(2,1)}, bf16[12,768,256]{2,1,0:T(8,128)(2,1)}, u32[]{:S(2)}, u32[]{:S(2)}) collective-permute-start(bf16[12,768,256]{2,1,0:T(8,128)(2,1)} %gather_fusion), channel_id=1, source_target_pairs={{1,0},{2,1},{3,2},{4,3},{5,4},{6,5},{7,6},{8,7},{9,8},{10,9},{11,1... | collective-permute-start | bytes 14155784 | tf_op jit(solution)/shard_map/ppermute | solution.py:26
  25.0 0.1 add_reduce_fusion
  25.1 0.1 select_reduce_fusion
  25.3 6.9 %gather_fusion.1 = bf16[12,768,256]{2,1,0:T(8,128)(2,1)} fusion(bf16[24,768,256]{2,1,0:T(8,128)(2,1)} %bitcast.89, s32[1024]{0:T(1024)S(1)} %pad_clamp_fusion.1), kind=kCustom, calls=%fused_computation.1 | custom fusion | bytes 9437232 | tf_op jit(solution)/shard_map/gather | solution.py:85
  32.4 0.1 fusion.8
  32.5 3.7 %convolution_convert_fusion = bf16[4,256,768]{2,1,0:T(8,128)(2,1)S(1)} fusion(bf16[4,256,768]{2,1,0:T(8,128)(2,1)S(1)} %copy-done, bf16[4,768,768]{2,1,0:T(8,128)(2,1)} %param.7), kind=kOutput, calls=%fused_computation.8 | convolution fusion | flops 1208745984 | bytes 7864320 | tf_op jit(solution)/shard_map/akr,ars->aks/dot_general | solution.py:71
  36.3 1.6 convolution_bitcast_fusion
  37.8 79.0 %collective-permute-done.1 = bf16[12,768,256]{2,1,0:T(8,128)(2,1)} collective-permute-done((bf16[12,768,256]{2,1,0:T(8,128)(2,1)}, bf16[12,768,256]{2,1,0:T(8,128)(2,1)}, u32[]{:S(2)}, u32[]{:S(2)}) %collective-permute-start.1) | collective-permute-done | bytes 4718624 | tf_op jit(solution)/shard_map/ppermute | solution.py:26
  116.9 7.8 %collective-permute-done.3 = bf16[12,768,256]{2,1,0:T(8,128)(2,1)} collective-permute-done((bf16[12,768,256]{2,1,0:T(8,128)(2,1)}, bf16[12,768,256]{2,1,0:T(8,128)(2,1)}, u32[]{:S(2)}, u32[]{:S(2)}) %collective-permute-start.3) | collective-permute-done | bytes 4718624 | tf_op jit(solution)/shard_map/ppermute | solution.py:26
  124.7 16.9 %pad_maximum_fusion = bf16[48,768,256]{2,1,0:T(8,128)(2,1)} fusion(bf16[12,768,256]{2,1,0:T(8,128)(2,1)} %collective-permute-done.3, bf16[12,768,256]{2,1,0:T(8,128)(2,1)} %collective-permute-done.1, bf16[24,768,256]{2,1,0:T(8,128)(2,1)} %bitcast.90), kind=kLoop, calls=%fused_computation.3 | loop fusion | flops 18874368 | bytes 37748736 | tf_op jit(solution)/shard_map/concatenate | solution.py:86
  141.6 12.3 %gather_fusion.2 = bf16[24,768,256]{2,1,0:T(8,128)(2,1)} fusion(bf16[48,768,256]{2,1,0:T(8,128)(2,1)} %pad_maximum_fusion, s32[1024]{0:T(1024)S(1)} %pad_clamp_fusion), kind=kCustom, calls=%fused_computation.2 | custom fusion | bytes 18874464 | tf_op jit(solution)/shard_map/gather | solution.py:87
  153.9 6.4 %fusion.1 = f32[4,256,6,256]{1,3,2,0:T(8,128)S(1)} fusion(bf16[4,6,768,256]{3,2,1,0:T(8,128)(2,1)} %bitcast.87, bf16[4,256,768]{2,1,0:T(8,128)(2,1)S(1)} %convolution_convert_fusion), kind=kOutput, calls=%fused_computation.9 | convolution fusion | flops 2415919104 | bytes 17301504 | tf_op jit(solution)/shard_map/akr,ajrc->akjc/dot_general | solution.py:88
  160.4 3.4 %pad_maximum_fusion.1 = f32[4,256,7,256]{1,3,2,0:T(8,128)} fusion(f32[4,256,6,256]{1,3,2,0:T(8,128)S(1)} %fusion.1, f32[4,256,1,256]{1,3,2,0:T(8,128)S(1)} %copy-done.2), kind=kLoop, calls=%fused_computation.4 | loop fusion | flops 1835008 | bytes 14680064 | tf_op jit(solution)/shard_map/concatenate | solution.py:90
  163.8 8.5 %copy.97 = f32[4,256,1792]{2,1,0:T(8,128)} copy(f32[4,256,1792]{1,2,0:T(8,128)} %bitcast.91) | data formatting | bytes 14680064 | tf_op jit(solution)/shard_map/reshape | solution.py:90
  172.3 4.9 %fusion = bf16[1,4,256,1792]{3,2,1,0:T(8,128)(2,1)S(1)} fusion(f32[4,256,1792]{2,1,0:T(8,128)} %copy.97, bf16[4,256,1792]{2,1,0:T(8,128)(2,1)} %param.9), kind=kLoop, calls=%fused_computation.6 | loop fusion | flops 5505024 | bytes 14680064 | tf_op jit(solution)/shard_map/reshape | solution.py:94
  177.2 2.8 copy.98
  180.0 56.6 %all_to_all.33 = bf16[1,4,256,1792]{3,1,0,2:T(4,128)(2,1)S(1)} all-to-all(bf16[1,4,256,1792]{3,1,0,2:T(4,128)(2,1)S(1)} %copy.98), channel_id=1, replica_groups=mesh['box'=32,'grp'=4] {'box'}, dimensions={2} | all-to-all | bytes 7340032 | tf_op jit(solution)/shard_map/all_to_all | solution.py:96
  236.7 0.4 copy.108
  237.1 0.5 copy.100
  237.6 47.0 %all_to_all.34 = bf16[32,4,8,1792]{3,2,1,0:T(8,128)(2,1)S(1)} all-to-all(bf16[32,4,8,1792]{3,2,1,0:T(8,128)(2,1)S(1)} %copy.100), channel_id=1, replica_groups=mesh['box'=32,'grp'=4] {'grp'}, dimensions={0} | all-to-all | bytes 7340032 | tf_op jit(solution)/shard_map/all_to_all | solution.py:95
  284.7 2.1 copy.101
  (29 shorter events, 0.5 us)
Async XLA Ops:
  0.0 32.5 %copy-start = (bf16[4,256,768]{2,1,0:T(8,128)(2,1)S(1)}, bf16[4,256,768]{2,1,0:T(8,128)(2,1)}, u32[]{:S(2)}) copy-start(bf16[4,256,768]{2,1,0:T(8,128)(2,1)} %param.6) | copy-start | bytes 4718596
  0.8 9.5 %collective-permute-start = (s32[4,6,2]{1,0,2:T(4,128)S(1)}, s32[4,6,2]{1,0,2:T(4,128)S(1)}, u32[]{:S(2)}, u32[]{:S(2)}) collective-permute-start(s32[4,6,2]{1,0,2:T(4,128)S(1)} %pad_add_fusion), channel_id=1, source_target_pairs={{0,1},{1,2},{2,3},{3,4},{4,5},{5,6},{6,7},{7,8},{8,9},{9,10},{10,1... | collective-permute-start | bytes 584 | tf_op jit(solution)/shard_map/ppermute | solution.py:15
  2.5 7.9 %collective-permute-start.2 = (s32[4,6,2]{1,0,2:T(4,128)S(1)}, s32[4,6,2]{1,0,2:T(4,128)S(1)}, u32[]{:S(2)}, u32[]{:S(2)}) collective-permute-start(s32[4,6,2]{1,0,2:T(4,128)S(1)} %pad_add_fusion), channel_id=1, source_target_pairs={{1,0},{2,1},{3,2},{4,3},{5,4},{6,5},{7,6},{8,7},{9,8},{10,9},{11,1... | collective-permute-start | bytes 584 | tf_op jit(solution)/shard_map/ppermute | solution.py:18
  17.9 99.0 %collective-permute-start.1 = (bf16[12,768,256]{2,1,0:T(8,128)(2,1)}, bf16[12,768,256]{2,1,0:T(8,128)(2,1)}, u32[]{:S(2)}, u32[]{:S(2)}) collective-permute-start(bf16[12,768,256]{2,1,0:T(8,128)(2,1)} %gather_fusion), channel_id=1, source_target_pairs={{1,0},{2,1},{3,2},{4,3},{5,4},{6,5},{7,6},{8,7},{9,8},{10,9},{11,1... | collective-permute-start | bytes 14155784 | tf_op jit(solution)/shard_map/ppermute | solution.py:26
  25.2 6.9 %copy-start.3 = (s32[4,6]{1,0:T(4,128)S(1)}, s32[4,6]{1,0:T(4,128)}, u32[]{:S(2)}) copy-start(s32[4,6]{1,0:T(4,128)} %param.10) | copy-start | bytes 292
  25.2 7.0 %copy-start.4 = (s32[4,6]{1,0:T(4,128)S(1)}, s32[4,6]{1,0:T(4,128)}, u32[]{:S(2)}) copy-start(s32[4,6]{1,0:T(4,128)} %param.11) | copy-start | bytes 292
  32.1 92.6 %collective-permute-start.3 = (bf16[12,768,256]{2,1,0:T(8,128)(2,1)}, bf16[12,768,256]{2,1,0:T(8,128)(2,1)}, u32[]{:S(2)}, u32[]{:S(2)}) collective-permute-start(bf16[12,768,256]{2,1,0:T(8,128)(2,1)} %gather_fusion.1), channel_id=1, source_target_pairs={{127,0},{0,1},{1,2},{2,3},{3,4},{4,5},{5,6},{6,7},{7,8},{8,9},{9,1... | collective-permute-start | bytes 14155784 | tf_op jit(solution)/shard_map/ppermute | solution.py:26
  153.9 6.5 %copy-start.2 = (f32[4,256,1,256]{1,3,2,0:T(8,128)S(1)}, f32[4,256,1,256]{1,3,2,0:T(8,128)}, u32[]{:S(2)}) copy-start(f32[4,256,1,256]{1,3,2,0:T(8,128)} %convolution_bitcast_fusion) | copy-start | bytes 3145732
  237.6 49.2 %copy-start.1 = (bf16[4,256,768]{2,1,0:T(8,128)(2,1)S(1)}, bf16[4,256,768]{2,1,0:T(8,128)(2,1)}, u32[]{:S(2)}) copy-start(bf16[4,256,768]{2,1,0:T(8,128)(2,1)} %param.6) | copy-start | bytes 4718596
where the time goes:
time: 288 us; the launch traced here: 287 us
  blocking collectives  104 us (36%)
  waiting for transfers between devices  88.2 us (31%)
  local copies, waits for them, and re-layouts  40.8 us (14%)
  other arithmetic  26.9 us (9%)
  starting transfers between devices  15.3 us (5%)
  matrix products  11.7 us (4%)
    ppermute x2, waiting for transfers between devices, from_behind(): return lax.ppermute(block, axis, route)  86.9 us
    all_to_all x1, blocking collectives, per_device(): lax.all_to_all(packed, 'box', split_axis=2, concat_axis=0, tiled=True)  56.6 us
    all_to_all x1, blocking collectives, per_device(): lax.all_to_all(lax.all_to_all(packed, 'box', split_axis=2, concat_axis=0,...  47 us
    concatenate x1, other arithmetic, per_device(): tile_pool = jnp.concatenate([tile_rows, from_after, from_before], axis=0)  16.9 us
    gather x1, local copies, waits for them, and re-layouts, per_device(): tile_pool[index].reshape(box_count, slot_count, red_rows, skel_rows)  12.3 us
    reshape x1, local copies, waits for them, and re-layouts, per_device(): jnp.concatenate([own_term[:, :, None, :], update], axis=2)  8.47 us
    ppermute x2, starting transfers between devices, from_behind(): return lax.ppermute(block, axis, route)  7.08 us
    gather x1, local copies, waits for them, and re-layouts, per_device(): from_before = from_behind(tile_rows[ahead_src], ('box', 'grp'), 1)  6.86 us
  transfers between devices with their start and end apart: 4, of which 3 were waited for; matrix products, arithmetic and copies ran while one was open for 5% of the time, Pallas kernels for 0%

commit v1 on v0

v1 whole, which is shorter than its diff:
```python
import functools

import jax
import jax.numpy as jnp
from jax import lax
from jax.experimental import pallas as pl
from jax.experimental.pallas import tpu as pltpu
from jax.sharding import PartitionSpec as P

FAR = 12
HALVES = 2
MESH = pl.DeviceIdType.MESH


def request_tables(neighbour, source_slot, device_now, device_count):
    box_count, slot_count = neighbour.shape
    total = box_count * slot_count
    boxes = neighbour.reshape(-1)
    owner = boxes // box_count
    place = (boxes - owner * box_count) * slot_count + source_slot.reshape(-1)
    asked = jnp.stack(
        [
            owner == (device_now + 1) % device_count,
            owner == (device_now + device_count - 1) % device_count,
        ]
    )
    order = jnp.arange(total, dtype=jnp.int32)
    before = (order[None, :] < order[:, None]).astype(jnp.int32)
    rank = jnp.sum(before[None] * asked[:, None, :].astype(jnp.int32), axis=2)
    lanes = jnp.arange(128, dtype=jnp.int32)
    onehot = jnp.logical_and(
        jnp.logical_and(rank[:, None, :] == lanes[None, :, None], lanes[None, :, None] < FAR), asked[:, None, :]
    ).astype(jnp.int32)
    tile_list = jnp.sum(onehot * place[None, None, :], axis=2)
    box_list = jnp.sum(onehot * (order // slot_count)[None, None, :], axis=2)
    lists = jnp.stack([tile_list, box_list] + [jnp.zeros_like(tile_list)] * 6, axis=1)
    here = jnp.logical_not(jnp.logical_or(asked[0], asked[1]))
    local_tile = jnp.where(here, place, total)
    result_at = jnp.where(asked[0], rank[0], jnp.where(asked[1], FAR + rank[1], 2 * FAR))
    return lists, jnp.stack([local_tile, result_at])


def kernel(
    groups, boxes_axis,
    table, lists, split_coupling, coupling, inverse, tiles, split_near,
    out,
    cp, inv, full_c, tile, base, own_w, wr0, wr1, rs0, rs1, res0, res1, ob0, ob1, stage, list_in, list_s,
    load_sem, list_send, list_recv, w_send, w_recv, r_send, r_recv, st_send, st_recv, out_send, out_recv,
):
    box_count, halves, half_rows, red = cp.shape
    skel = halves * half_rows
    slots = 6
    total = box_count * slots
    per_group = boxes_axis // groups
    z_count = per_group // 2
    z_half = z_count // 2
    dests = boxes_axis // 2
    wr, rs, res, ob = (wr0, wr1), (rs0, rs1), (res0, res1), (ob0, ob1)
    b = lax.axis_index("box")
    g = lax.axis_index("grp")
    x = b // per_group
    z = (b % per_group) // 2
    c = b % 2
    count = boxes_axis * groups
    here = b * groups + g
    after = lax.rem(here + 1, count)
    behind = lax.rem(here + count - 1, count)
    near_devices = ((after // groups, after % groups), (behind // groups, behind % groups))
    parity = [lax.rem(z + h, 2) for h in range(halves)]

    barrier = pltpu.get_barrier_semaphore()

    def greet(k, carry):
        pl.semaphore_signal(barrier, inc=1, device_id=(lax.rem(b + k, boxes_axis), g), device_id_type=MESH)
        return carry

    lax.fori_loop(1, boxes_axis, greet, 0)
    for k in range(1, groups):
        pl.semaphore_signal(barrier, inc=1, device_id=(b, lax.rem(g + k, groups)), device_id_type=MESH)
    for device in near_devices:
        pl.semaphore_signal(barrier, inc=1, device_id=device, device_id_type=MESH)

    def load_c(a, h):
        return pltpu.make_async_copy(
            split_coupling.at[a, :, :, parity[h]], cp6.at[a, h], load_sem.at[a * 3 + h]
        )

    cp6 = cp.reshape(box_count, halves, groups, z_half, 16, red)
    near6 = base.reshape(box_count, halves, groups, z_half, 16, base.shape[-1])

    def load_inv(a):
        return pltpu.make_async_copy(inverse.at[a], inv.at[a], load_sem.at[a * 3 + 2])

    for a in range(box_count):
        for h in range(halves):
            load_c(a, h).start()
        load_inv(a).start()
    first = 3 * box_count
    rest = [
        pltpu.make_async_copy(coupling, full_c, load_sem.at[first]),
        pltpu.make_async_copy(tiles, tile.at[pl.ds(0, total)], load_sem.at[first + 1]),
    ] + [
        pltpu.make_async_copy(split_near.at[:, :, :, parity[h]], near6.at[:, h], load_sem.at[first + 2 + h])
        for h in range(halves)
    ]
    for copy in rest:
        copy.start()
    tile[total] = jnp.zeros_like(tile[total])
    for h in range(halves):
        res[h][2 * FAR] = jnp.zeros_like(res[h][2 * FAR])

    pl.semaphore_wait(barrier, boxes_axis - 1 + groups - 1 + 2)

    list_copies = [
        pltpu.make_async_remote_copy(
            src_ref=lists.at[d],
            dst_ref=list_in.at[1 - d],
            send_sem=list_send.at[d],
            recv_sem=list_recv.at[1 - d],
            device_id=near_devices[d],
            device_id_type=MESH,
        )
        for d in range(2)
    ]
    for copy in list_copies:
        copy.start()

    def send_w(a, h):
        for d in range(2):
            pltpu.make_async_remote_copy(
                src_ref=own_w.at[a, h],
                dst_ref=wr[h].at[1 - d, a],
                send_sem=w_send.at[h, d],
                recv_sem=w_recv.at[h, 1 - d],
                device_id=near_devices[d],
                device_id_type=MESH,
            ).start()

    def weights(a, carry):
        for h in range(halves):
            load_c(a, h).wait()
        load_inv(a).wait()
        product = jnp.dot(cp[a].reshape(skel, red), inv[a], preferred_element_type=jnp.float32)
        own_w[a] = product.astype(jnp.bfloat16).reshape(halves, half_rows, red)
        send_w(a, 0)
        return carry

    lax.fori_loop(0, box_count, weights, 0)

    for copy in rest:
        copy.wait()

    def local_terms(a, carry):
        w = own_w[a].reshape(skel, red)
        own = lax.dot_general(w, full_c[a], (((1,), (1,)), ((), ())), preferred_element_type=jnp.float32)
        cols = pl.ds(0, skel)
        near = base[a, :, :, cols].reshape(skel, skel).astype(jnp.float32)
        base[a, :, :, cols] = (near - own).astype(jnp.bfloat16).reshape(halves, half_rows, skel)
        for j in range(slots):
            cols = pl.ds((j + 1) * skel, skel)
            pair = jnp.dot(w, tile[table[0, a * slots + j]], preferred_element_type=jnp.float32)
            near = base[a, :, :, cols].reshape(skel, skel).astype(jnp.float32)
            base[a, :, :, cols] = (near - pair).astype(jnp.bfloat16).reshape(halves, half_rows, skel)
        return carry

    lax.fori_loop(0, box_count, local_terms, 0)

    for copy in list_copies:
        copy.wait()
    to_scalars = pltpu.make_async_copy(list_in, list_s, load_sem.at[first + 2 + halves])
    to_scalars.start()
    to_scalars.wait()

    def remote_terms(h):
        for d in range(2):
            pltpu.make_async_copy(wr[h].at[d], wr[h].at[d], w_recv.at[h, d]).wait()

        def one(k, carry):
            for d in range(2):
                pair = jnp.dot(
                    wr[h][d, list_s[d, 1, k]], tile[list_s[d, 0, k]], preferred_element_type=jnp.float32
                )
                rs[h][d, k] = pair.astype(jnp.bfloat16)
                pltpu.make_async_remote_copy(
                    src_ref=rs[h].at[d, k],
                    dst_ref=res[h].at[(1 - d) * FAR + k],
                    send_sem=r_send.at[h, d],
                    recv_sem=r_recv.at[h, 1 - d],
                    device_id=near_devices[d],
                    device_id_type=MESH,
                ).start()
            return carry

        lax.fori_loop(0, FAR, one, 0)

    def finish(h):
        for d in range(2):
            arrived = res[h].at[pl.ds(d * FAR, FAR)]
            pltpu.make_async_copy(arrived, arrived, r_recv.at[h, d]).wait()

        def one(a, carry):
            ob[h][:, a, :, pl.ds(0, skel)] = base[a, h, :, pl.ds(0, skel)].reshape(dests, 8, skel)
            for j in range(slots):
                cols = pl.ds((j + 1) * skel, skel)
                value = base[a, h, :, cols].astype(jnp.float32) - res[h][table[1, a * slots + j]].astype(jnp.float32)
                ob[h][:, a, :, cols] = value.reshape(dests, 8, skel).astype(jnp.bfloat16)
            return carry

        lax.fori_loop(0, box_count, one, 0)

    def spread(h):
        def slot(dx, dz, dc):
            to_x = lax.rem(x + dx, groups)
            to_z = lax.rem(z + h + 2 * dz, z_count)
            to_c = lax.rem(c + dc, 2)
            return (to_x * z_half + to_z // 2) * 2 + to_c, to_x * per_group + to_z * 2 + to_c

        def send(s, carry):
            place, to_b = slot(s % groups, (s // groups) % z_half, s // (groups * z_half))
            pltpu.make_async_remote_copy(
                src_ref=ob[h].at[place],
                dst_ref=stage.at[x, z // 2, lax.rem(z, 2), c],
                send_sem=st_send.at[h],
                recv_sem=st_recv.at[h, x],
                device_id=(to_b, g),
                device_id_type=MESH,
            ).start()
            return carry

        if h == 0:
            place, _ = slot(0, 0, 0)
            pltpu.make_async_copy(
                ob[h].at[place], stage.at[x, z // 2, lax.rem(z, 2), c], st_recv.at[h, x]
            ).start()
        lax.fori_loop(1 if h == 0 else 0, dests, send, 0)

    def forward(h):
        for step in (0, 1, 3, 2):
            from_x = lax.rem(x + step, groups)
            piece = stage.at[from_x, :, parity[h]]
            pltpu.make_async_copy(piece, piece, st_recv.at[h, from_x]).wait()
            place = out.at[:, parity[h], :, g]

            @pl.when(from_x == g)
            def _():
                pltpu.make_async_copy(piece, place, out_recv).start()

            @pl.when(from_x != g)
            def _():
                pltpu.make_async_remote_copy(
                    src_ref=piece,
                    dst_ref=place,
                    send_sem=out_send.at[h],
                    recv_sem=out_recv,
                    device_id=(b, from_x),
                    device_id_type=MESH,
                ).start()

    def send_w_half(h):
        def one(a, carry):
            send_w(a, h)
            return carry

        lax.fori_loop(0, box_count, one, 0)

    remote_terms(0)
    send_w_half(1)
    remote_terms(1)
    finish(0)
    spread(0)
    forward(0)
    finish(1)
    spread(1)
    forward(1)

    pltpu.make_async_copy(out, out, out_recv).wait()
    for h in range(halves):
        for d in range(2):
            pltpu.make_async_copy(wr[h].at[d], wr[h].at[d], w_send.at[h, d]).wait()
            pltpu.make_async_copy(rs[h].at[d], rs[h].at[d], r_send.at[h, d]).wait()
        sent = ob[h].at[pl.ds(0, dests - 1 if h == 0 else dests)]
        pltpu.make_async_copy(sent, sent, st_send.at[h]).wait()
        sent = stage.at[pl.ds(0, groups - 1), :, 0]
        pltpu.make_async_copy(sent, sent, out_send.at[h]).wait()


def per_device(groups, boxes_axis, coupling, inverse, tiles, near_block, neighbour, source_slot):
    box_count, skel, red = coupling.shape
    slots = neighbour.shape[1]
    total = box_count * slots
    width = near_block.shape[-1]
    rows = skel // boxes_axis
    half_rows = skel // HALVES
    z_half = boxes_axis // groups // 4
    device_now = lax.axis_index(("box", "grp"))
    lists, table = request_tables(neighbour, source_slot, device_now, boxes_axis * groups)
    half = jnp.bfloat16
    split = (box_count, groups, z_half, 2, 2 * rows)
    dests = boxes_axis // 2
    hbm = pl.BlockSpec(memory_space=pl.ANY)
    moved = pl.pallas_call(
        functools.partial(kernel, groups, boxes_axis),
        out_shape=jax.ShapeDtypeStruct((z_half, 2, 2, groups, box_count, rows, width), half),
        in_specs=[
            pl.BlockSpec(memory_space=pltpu.SMEM),
            pl.BlockSpec(memory_space=pltpu.VMEM),
            hbm, hbm, hbm, hbm, hbm,
        ],
        out_specs=hbm,
        scratch_shapes=[
            pltpu.VMEM((box_count, HALVES, half_rows, red), half),
            pltpu.VMEM((box_count, red, red), half),
            pltpu.VMEM((box_count, skel, red), half),
            pltpu.VMEM((total + 1, red, skel), half),
            pltpu.VMEM((box_count, HALVES, half_rows, width), half),
            pltpu.VMEM((box_count, HALVES, half_rows, red), half),
        ]
        + [pltpu.VMEM((2, box_count, half_rows, red), half)] * 2
        + [pltpu.VMEM((2, FAR, half_rows, skel), half)] * 2
        + [pltpu.VMEM((2 * FAR + 1, half_rows, skel), half)] * 2
        + [pltpu.VMEM((dests, box_count, rows, width), half)] * 2
        + [
            pltpu.VMEM((groups, z_half, 2, 2, box_count, rows, width), half),
            pltpu.VMEM(lists.shape, jnp.int32),
            pltpu.SMEM(lists.shape, jnp.int32),
            pltpu.SemaphoreType.DMA((3 * box_count + 3 + HALVES,)),
            pltpu.SemaphoreType.DMA((2,)),
            pltpu.SemaphoreType.DMA((2,)),
            pltpu.SemaphoreType.DMA((HALVES, 2)),
            pltpu.SemaphoreType.DMA((HALVES, 2)),
            pltpu.SemaphoreType.DMA((HALVES, 2)),
            pltpu.SemaphoreType.DMA((HALVES, 2)),
            pltpu.SemaphoreType.DMA((HALVES,)),
            pltpu.SemaphoreType.DMA((HALVES, groups)),
            pltpu.SemaphoreType.DMA((HALVES,)),
            pltpu.SemaphoreType.DMA,
        ],
        compiler_params=pltpu.CompilerParams(
            collective_id=0, has_side_effects=True, vmem_limit_bytes=56 * 2**20
        ),
        cost_estimate=pl.CostEstimate(flops=9 * 10**9, bytes_accessed=24 * 10**6, transcendentals=0),
    )(
        table,
        lists,
        coupling.reshape(split + (red,)),
        coupling,
        inverse,
        tiles.reshape(total, red, skel),
        near_block.reshape(split + (width,)),
    )
    return moved.reshape(-1, rows, width)


def solution(mesh):
    return jax.shard_map(
        functools.partial(per_device, mesh.shape["grp"], mesh.shape["box"]),
        mesh=mesh,
        in_specs=(
            P(("box", "grp"), None, None),
            P(("box", "grp"), None, None),
            P(("box", "grp"), None, None, None),
            P(("box", "grp"), None, None),
            P(("box", "grp"), None),
            P(("box", "grp"), None),
        ),
        out_specs=P("grp", "box", None),
        check_vma=False,
    )
```

time: 288 us -> 157 us (0.55)
  the two profiles are of different devices: /device:TPU:0 before, /device:TPU:48 now
where the time goes in v1:
time: 157 us
  Pallas kernels  148 us (94%)
  local copies, waits for them, and re-layouts  7.32 us (5%)
    pallas_call x1, Pallas kernels, per_device(): pl.pallas_call(functools.partial(kernel, groups, boxes_axis), out_shape=j...  148 us
    unnamed x1, local copies, waits for them, and re-layouts  4.11 us

profile of v1, /device:TPU:48, one launch (start us, length us, event | category | flops | bytes accessed | tf_op | source)
XLA Modules:
  0.0 157.1 jit_solution(5471688904678299024)
XLA Ops:
  0.0 0.8 reshape.258
  0.8 0.8 reshape.256
  1.5 0.8 reshape.259
  2.3 0.8 reshape.257
  3.1 0.1 pad.3.clone
  3.2 0.1 pad.2.clone
  3.3 0.1 multiply_reduce_fusion
  3.4 0.1 select_reduce_fusion.1
  3.5 0.6 pad_add_fusion.1.table
  4.1 0.7 add_add_fusion.lists
  4.8 148.2 %shard_map.64 = bf16[2,2,2,4,4,8,1792]{6,5,4,3,2,1,0:T(8,128)(2,1)} custom-call(s32[2,24]{1,0:T(2,128)} %pad_add_fusion.1.table, s32[2,8,128]{2,1,0:T(8,128)} %add_add_fusion.lists, bf16[4,4,2,2,16,768]{5,4,3,2,1,0:T(8,128)(2,1)} %bitcast.11, bf16[4,256,768]{2,1,0:T(8,128)(2,1)} %coupling.1, bf16[4,768,768]{2,1,0:T(8,128)(2,1)} %inverse.1, ...), custom_call_target="tpu_custom_call" | custom-call | flops 8999999488 | bytes 24000000 | tf_op jit(solution)/shard_map/pallas_call | solution.py:301
  152.9 4.1 %copy.8 = bf16[128,8,1792]{2,1,0:T(8,128)(2,1)} copy(bf16[128,8,1792]{2,1,0:T(8,128)(2,1)} %bitcast.6) | data formatting | bytes 7340032
  (8 shorter events, 0.1 us)

commit v2 on v1

v2 whole, which is shorter than its diff:
```python
import functools

import jax
import jax.numpy as jnp
from jax import lax
from jax.experimental import pallas as pl
from jax.experimental.pallas import tpu as pltpu
from jax.sharding import PartitionSpec as P

FAR = 12
GROUP = 3
MESH = pl.DeviceIdType.MESH


def request_tables(neighbour, source_slot, device_now, device_count):
    box_count, slot_count = neighbour.shape
    total = box_count * slot_count
    order = jnp.arange(total, dtype=jnp.int32)
    spot = (jnp.arange(box_count)[:, None] * slot_count + jnp.arange(slot_count)[None, :]).astype(jnp.int32)
    picks = (spot[None] == order[:, None, None]).astype(jnp.int32)
    flat = jnp.sum(picks * (neighbour * slot_count + source_slot)[None], axis=(1, 2))
    owner = flat // total
    place = flat - owner * total
    asked = jnp.stack(
        [
            owner == (device_now + 1) % device_count,
            owner == (device_now + device_count - 1) % device_count,
        ]
    )
    before = (order[None, :] < order[:, None]).astype(jnp.int32)
    rank = jnp.sum(before[None] * asked[:, None, :].astype(jnp.int32), axis=2)
    lanes = jnp.arange(128, dtype=jnp.int32)
    onehot = jnp.logical_and(
        jnp.logical_and(rank[:, None, :] == lanes[None, :, None], lanes[None, :, None] < FAR), asked[:, None, :]
    ).astype(jnp.int32)
    tile_list = jnp.sum(onehot * place[None, None, :], axis=2)
    box_list = jnp.sum(onehot * (order // slot_count)[None, None, :], axis=2)
    here = jnp.logical_not(jnp.logical_or(asked[0], asked[1]))
    local_tile = jnp.where(here, place, total)
    result_at = jnp.where(asked[0], rank[0], jnp.where(asked[1], FAR + rank[1], 2 * FAR))
    own = jnp.pad(jnp.stack([local_tile, result_at]), ((0, 0), (0, 128 - total)))
    rows = jnp.stack([jnp.stack([tile_list[0], box_list[0]]), jnp.stack([tile_list[1], box_list[1]]), own])
    return jnp.pad(rows, ((0, 0), (0, 6), (0, 0)))


def kernel(
    groups, boxes_axis, chunks, slots,
    lists, split_coupling, coupling, inverse, tiles, split_near,
    out,
    cp, inv, full_c, tile, base, own_w, stage, list_in, list_s,
    load_sem, c_sem, near_sem, list_send, list_recv, w_send, w_recv, r_send, r_recv,
    st_send, st_recv, out_send, out_recv, *buffers,
):
    box_count, skel, red = cp.shape
    total = box_count * slots
    per_group = boxes_axis // groups
    z_count = chunks
    piece_rows = 16
    chunk_rows = groups * piece_rows
    dests = groups * 2
    wr, rs, res, ob = (buffers[n * chunks : (n + 1) * chunks] for n in range(4))
    b = lax.axis_index("box")
    g = lax.axis_index("grp")
    x = b // per_group
    z = (b % per_group) // 2
    c = b % 2
    count = boxes_axis * groups
    here = b * groups + g
    after = lax.rem(here + 1, count)
    behind = lax.rem(here + count - 1, count)
    beside = ((after // groups, after % groups), (behind // groups, behind % groups))

    def to_xz(q, dx):
        return lax.rem(x + dx, groups), lax.rem(z + q - dx + 2 * z_count, z_count)

    def load_c(q, dx):
        to_x, to_z = to_xz(q, dx)
        rows = pl.ds((q * groups + dx) * piece_rows, piece_rows)
        return pltpu.make_async_copy(split_coupling.at[:, to_x, to_z], cp.at[:, rows], c_sem.at[q * groups + dx])

    def load_near(q, dx):
        to_x, to_z = to_xz(q, dx)
        rows = pl.ds(dx * piece_rows, piece_rows)
        return pltpu.make_async_copy(
            split_near.at[:, to_x, to_z], base.at[q, :, rows], near_sem.at[q * groups + dx]
        )

    def load_inv(a):
        return pltpu.make_async_copy(inverse.at[a], inv.at[a], load_sem.at[a])

    pieces = [(q, dx) for q in range(chunks) for dx in range(groups)]
    for q, dx in pieces:
        load_c(q, dx).start()
    for a in range(box_count):
        load_inv(a).start()
    barrier = pltpu.get_barrier_semaphore()

    def greet(k, carry):
        pl.semaphore_signal(barrier, inc=1, device_id=(lax.rem(b + k, boxes_axis), g), device_id_type=MESH)
        return carry

    lax.fori_loop(1, boxes_axis, greet, 0)
    for k in range(1, groups):
        pl.semaphore_signal(barrier, inc=1, device_id=(b, lax.rem(g + k, groups)), device_id_type=MESH)
    for device in beside:
        pl.semaphore_signal(barrier, inc=1, device_id=device, device_id_type=MESH)

    load_tiles = pltpu.make_async_copy(tiles, tile.at[pl.ds(0, total)], load_sem.at[box_count])
    load_full = pltpu.make_async_copy(coupling, full_c, load_sem.at[box_count + 1])
    load_own = pltpu.make_async_copy(lists.at[2], list_s.at[2], load_sem.at[box_count + 2])
    load_full.start()
    load_tiles.start()
    for q, dx in pieces:
        load_near(q, dx).start()
    load_own.start()
    tile[total] = jnp.zeros_like(tile[total])
    for q in range(chunks):
        res[q][2 * FAR] = jnp.zeros_like(res[q][2 * FAR])

    def send_w(q, a):
        for d in range(2):
            pltpu.make_async_remote_copy(
                src_ref=own_w.at[q, a],
                dst_ref=wr[q].at[1 - d, a],
                send_sem=w_send.at[q, d],
                recv_sem=w_recv.at[q, 1 - d],
                device_id=beside[d],
                device_id_type=MESH,
            ).start()

    def send_w_all(q):
        def one(a, carry):
            send_w(q, a)
            return carry

        lax.fori_loop(0, box_count, one, 0)

    for q, dx in pieces:
        load_c(q, dx).wait()

    def weights(a, carry):
        load_inv(a).wait()
        product = jnp.dot(cp[a], inv[a], preferred_element_type=jnp.float32)
        own_w[:, a] = product.astype(jnp.bfloat16).reshape(chunks, chunk_rows, red)
        return carry

    lax.fori_loop(0, 1, weights, 0)
    pl.semaphore_wait(barrier, boxes_axis - 1 + groups - 1 + 2)

    def weights_sent(a, carry):
        send_w(0, a)

        @pl.when(a + 1 < box_count)
        def _():
            weights(a + 1, 0)

        return carry

    lax.fori_loop(0, box_count, weights_sent, 0)
    send_w_all(1)
    list_copies = [
        pltpu.make_async_remote_copy(
            src_ref=lists.at[d],
            dst_ref=list_in.at[1 - d],
            send_sem=list_send.at[d],
            recv_sem=list_recv.at[1 - d],
            device_id=beside[d],
            device_id_type=MESH,
        )
        for d in range(2)
    ]
    for copy in list_copies:
        copy.start()


    load_full.wait()
    load_tiles.wait()
    for q, dx in pieces:
        load_near(q, dx).wait()
    load_own.wait()

    def local_terms(a, carry):
        w = own_w[:, a].reshape(skel, red)
        own = lax.dot_general(w, full_c[a], (((1,), (1,)), ((), ())), preferred_element_type=jnp.float32)
        cols = pl.ds(0, skel)
        near = base[:, a, :, cols].reshape(skel, skel).astype(jnp.float32)
        base[:, a, :, cols] = (near - own).astype(jnp.bfloat16).reshape(chunks, chunk_rows, skel)
        for j in range(slots):
            cols = pl.ds((j + 1) * skel, skel)
            pair = jnp.dot(w, tile[list_s[2, 0, a * slots + j]], preferred_element_type=jnp.float32)
            near = base[:, a, :, cols].reshape(skel, skel).astype(jnp.float32)
            base[:, a, :, cols] = (near - pair).astype(jnp.bfloat16).reshape(chunks, chunk_rows, skel)
        return carry

    lax.fori_loop(0, box_count, local_terms, 0)

    for copy in list_copies:
        copy.wait()
    to_scalars = pltpu.make_async_copy(list_in, list_s.at[pl.ds(0, 2)], load_sem.at[box_count + 3])
    to_scalars.start()
    to_scalars.wait()

    def remote_terms(q):
        for d in range(2):
            pltpu.make_async_copy(wr[q].at[d], wr[q].at[d], w_recv.at[q, d]).wait()

        def one(n, carry):
            for d in range(2):
                for i in range(GROUP):
                    k = n * GROUP + i
                    pair = jnp.dot(
                        wr[q][d, list_s[d, 1, k]], tile[list_s[d, 0, k]], preferred_element_type=jnp.float32
                    )
                    rs[q][d, k] = pair.astype(jnp.bfloat16)
                pltpu.make_async_remote_copy(
                    src_ref=rs[q].at[d, pl.ds(n * GROUP, GROUP)],
                    dst_ref=res[q].at[pl.ds((1 - d) * FAR + n * GROUP, GROUP)],
                    send_sem=r_send.at[q, d],
                    recv_sem=r_recv.at[q, 1 - d],
                    device_id=beside[d],
                    device_id_type=MESH,
                ).start()
            return carry

        lax.fori_loop(0, FAR // GROUP, one, 0)

    def finish(q):
        for d in range(2):
            arrived = res[q].at[pl.ds(d * FAR, FAR)]
            pltpu.make_async_copy(arrived, arrived, r_recv.at[q, d]).wait()

        def one(a, carry):
            ob[q][:, a, :, pl.ds(0, skel)] = base[q, a, :, pl.ds(0, skel)].reshape(dests, 8, skel)
            for j in range(slots):
                cols = pl.ds((j + 1) * skel, skel)
                value = base[q, a, :, cols].astype(jnp.float32) - res[q][list_s[2, 1, a * slots + j]].astype(jnp.float32)
                ob[q][:, a, :, cols] = value.reshape(dests, 8, skel).astype(jnp.bfloat16)
            return carry

        lax.fori_loop(0, box_count, one, 0)

        def send(s, carry):
            dx, to_c = s % groups, lax.rem(c + s // groups, 2)
            to_x, to_z = to_xz(q, dx)
            pltpu.make_async_remote_copy(
                src_ref=ob[q].at[dx * 2 + to_c],
                dst_ref=stage.at[x, z, c],
                send_sem=st_send.at[q],
                recv_sem=st_recv.at[q, x],
                device_id=(to_x * per_group + to_z * 2 + to_c, g),
                device_id_type=MESH,
            ).start()
            return carry

        if q == 0:
            pltpu.make_async_copy(ob[q].at[c], stage.at[x, z, c], st_recv.at[q, x]).start()
        lax.fori_loop(1 if q == 0 else 0, dests, send, 0)

    def forward(q):
        for step in (0, 1, 3, 2):
            from_x = lax.rem(x + step, groups)
            from_z = lax.rem(z - q + lax.rem(groups - step, groups) + 2 * z_count, z_count)
            piece = stage.at[from_x, from_z]
            pltpu.make_async_copy(piece, piece, st_recv.at[q, from_x]).wait()
            place = out.at[from_z, :, g]

            @pl.when(from_x == g)
            def _():
                pltpu.make_async_copy(piece, place, out_recv).start()

            @pl.when(from_x != g)
            def _():
                pltpu.make_async_remote_copy(
                    src_ref=piece,
                    dst_ref=place,
                    send_sem=out_send.at[q],
                    recv_sem=out_recv,
                    device_id=(b, from_x),
                    device_id_type=MESH,
                ).start()

    plan = PLAN
    steps = {"t": remote_terms, "w": send_w_all, "f": finish, "o": forward}
    for step in plan.split():
        steps[step[0]](int(step[1:]))

    pltpu.make_async_copy(out, out, out_recv).wait()
    for q in range(chunks):
        for d in range(2):
            pltpu.make_async_copy(wr[q].at[d], wr[q].at[d], w_send.at[q, d]).wait()
            pltpu.make_async_copy(rs[q].at[d], rs[q].at[d], r_send.at[q, d]).wait()
        sent = ob[q].at[pl.ds(0, dests - 1 if q == 0 else dests)]
        pltpu.make_async_copy(sent, sent, st_send.at[q]).wait()
        sent = stage.at[pl.ds(0, groups - 1), 0]
        pltpu.make_async_copy(sent, sent, out_send.at[q]).wait()


PLAN = "t0 w2 t1 w3 f0 t2 f1 o0 t3 f2 o1 f3 o2 o3"


def per_device(groups, boxes_axis, coupling, inverse, tiles, near_block, neighbour, source_slot):
    box_count, skel, red = coupling.shape
    slots = neighbour.shape[1]
    total = box_count * slots
    width = near_block.shape[-1]
    rows = skel // boxes_axis
    chunks = boxes_axis // groups // 2
    chunk_rows = skel // chunks
    device_now = lax.axis_index(("box", "grp"))
    lists = request_tables(neighbour, source_slot, device_now, boxes_axis * groups)
    half = jnp.bfloat16
    split = (box_count, groups, chunks, 2 * rows)
    hbm = pl.BlockSpec(memory_space=pltpu.HBM)
    moved = pl.pallas_call(
        functools.partial(kernel, groups, boxes_axis, chunks, slots),
        out_shape=jax.ShapeDtypeStruct((chunks, 2, groups, box_count, rows, width), half),
        in_specs=[pl.BlockSpec(memory_space=pltpu.VMEM), hbm, hbm, hbm, hbm, hbm],
        out_specs=pl.BlockSpec(memory_space=pl.ANY),
        scratch_shapes=[
            pltpu.VMEM((box_count, skel, red), half),
            pltpu.VMEM((box_count, red, red), half),
            pltpu.VMEM((box_count, skel, red), half),
            pltpu.VMEM((total + 1, red, skel), half),
            pltpu.VMEM((chunks, box_count, chunk_rows, width), half),
            pltpu.VMEM((chunks, box_count, chunk_rows, red), half),
            pltpu.VMEM((groups, chunks, 2, box_count, rows, width), half),
            pltpu.VMEM((2,) + lists.shape[1:], jnp.int32),
            pltpu.SMEM(lists.shape, jnp.int32),
            pltpu.SemaphoreType.DMA((box_count + 4,)),
            pltpu.SemaphoreType.DMA((chunks * groups,)),
            pltpu.SemaphoreType.DMA((chunks * groups,)),
            pltpu.SemaphoreType.DMA((2,)),
            pltpu.SemaphoreType.DMA((2,)),
            pltpu.SemaphoreType.DMA((chunks, 2)),
            pltpu.SemaphoreType.DMA((chunks, 2)),
            pltpu.SemaphoreType.DMA((chunks, 2)),
            pltpu.SemaphoreType.DMA((chunks, 2)),
            pltpu.SemaphoreType.DMA((chunks,)),
            pltpu.SemaphoreType.DMA((chunks, groups)),
            pltpu.SemaphoreType.DMA((chunks,)),
            pltpu.SemaphoreType.DMA,
        ]
        + [pltpu.VMEM((2, box_count, chunk_rows, red), half)] * chunks
        + [pltpu.VMEM((2, FAR, chunk_rows, skel), half)] * chunks
        + [pltpu.VMEM((2 * FAR + 1, chunk_rows, skel), half)] * chunks
        + [pltpu.VMEM((2 * groups, box_count, rows, width), half)] * chunks,
        compiler_params=pltpu.CompilerParams(
            collective_id=0, has_side_effects=True, vmem_limit_bytes=46 * 2**20
        ),
        cost_estimate=pl.CostEstimate(flops=9 * 10**9, bytes_accessed=24 * 10**6, transcendentals=0),
    )(
        lists,
        coupling.reshape(split + (red,)),
        coupling,
        inverse,
        tiles.reshape(total, red, skel),
        near_block.reshape(split + (width,)),
    )
    return moved.reshape(-1, rows, width)


def solution(mesh):
    return jax.shard_map(
        functools.partial(per_device, mesh.shape["grp"], mesh.shape["box"]),
        mesh=mesh,
        in_specs=(
            P(("box", "grp"), None, None),
            P(("box", "grp"), None, None),
            P(("box", "grp"), None, None, None),
            P(("box", "grp"), None, None),
            P(("box", "grp"), None),
            P(("box", "grp"), None),
        ),
        out_specs=P("grp", "box", None),
        check_vma=False,
    )
```

time: 157 us -> 128 us (0.82)
  the two profiles are of different devices: /device:TPU:48 before, /device:TPU:0 now
where the time goes in v2:
time: 128 us; the launch traced here: 127 us
  Pallas kernels  122 us (95%)
  local copies, waits for them, and re-layouts  3.35 us (3%)
    pallas_call x1, Pallas kernels, per_device(): pl.pallas_call(functools.partial(kernel, groups, boxes_axis, chunks, slot...  122 us
    unnamed x3, local copies, waits for them, and re-layouts  3.24 us

profile of v2, /device:TPU:0, one launch (start us, length us, event | category | flops | bytes accessed | tf_op | source)
XLA Modules:
  0.0 126.8 jit_solution(7361120399223105564)
XLA Ops:
  0.0 0.7 multiply_add_fusion
  0.7 0.1 copy.7
  0.8 0.1 select_reduce_fusion.2
  1.0 0.1 multiply_reduce_fusion
  1.1 0.1 select_reduce_fusion.1
  1.3 0.0 copy-start
  1.3 1.4 %copy-done = bf16[4,256,768]{2,1,0:T(8,128)(2,1)S(1)} copy-done((bf16[4,256,768]{2,1,0:T(8,128)(2,1)S(1)}, bf16[4,256,768]{2,1,0:T(8,128)(2,1)}, u32[]{:S(2)}) %copy-start) | copy-done | bytes 1572888
  2.7 122.2 %shard_map.64 = bf16[4,2,4,4,8,1792]{5,4,3,2,1,0:T(8,128)(2,1)S(1)} custom-call(s32[3,8,128]{2,1,0:T(8,128)S(1)} %pad.9.lists, bf16[4,4,4,16,768]{4,3,2,1,0:T(8,128)(2,1)S(1)} %bitcast.30, bf16[4,256,768]{2,1,0:T(8,128)(2,1)S(1)} %copy-done, bf16[4,768,768]{2,1,0:T(8,128)(2,1)} %inverse.1, bf16[24,768,256]{2,1,0:T(8,128)(2,1)} %bitcast.31, ...), custom_call_target="tpu_custom_call" | custom-call | flops 8999999488 | bytes 24000000 | tf_op jit(solution)/shard_map/pallas_call | solution.py:314
  124.9 1.8 %copy.9 = bf16[128,8,1792]{2,1,0:T(8,128)(2,1)} copy(bf16[128,8,1792]{2,1,0:T(8,128)(2,1)S(1)} %bitcast.29) | data formatting | bytes 7340032
  (16 shorter events, 0.1 us)
Async XLA Ops:
  1.3 1.4 %copy-start = (bf16[4,256,768]{2,1,0:T(8,128)(2,1)S(1)}, bf16[4,256,768]{2,1,0:T(8,128)(2,1)}, u32[]{:S(2)}) copy-start(bf16[4,256,768]{2,1,0:T(8,128)(2,1)} %coupling.1) | copy-start | bytes 4718596

commit v3 on v2

--- a/solution.py
+++ b/solution.py
@@ -157,7 +157,6 @@
         return carry
 
     lax.fori_loop(0, box_count, weights_sent, 0)
-    send_w_all(1)
     list_copies = [
         pltpu.make_async_remote_copy(
             src_ref=lists.at[d],
@@ -193,6 +192,7 @@
         return carry
 
     lax.fori_loop(0, box_count, local_terms, 0)
+    send_w_all(1)
 
     for copy in list_copies:
         copy.wait()
@@ -279,10 +279,11 @@
                     device_id_type=MESH,
                 ).start()
 
-    plan = PLAN
-    steps = {"t": remote_terms, "w": send_w_all, "f": finish, "o": forward}
-    for step in plan.split():
-        steps[step[0]](int(step[1:]))
+    for step, q in (
+        (remote_terms, 0), (send_w_all, 2), (remote_terms, 1), (send_w_all, 3), (finish, 0), (remote_terms, 2),
+        (finish, 1), (forward, 0), (remote_terms, 3), (finish, 2), (forward, 1), (finish, 3), (forward, 2), (forward, 3),
+    ):
+        step(q)
 
     pltpu.make_async_copy(out, out, out_recv).wait()
     for q in range(chunks):
@@ -293,9 +294,6 @@
         pltpu.make_async_copy(sent, sent, st_send.at[q]).wait()
         sent = stage.at[pl.ds(0, groups - 1), 0]
         pltpu.make_async_copy(sent, sent, out_send.at[q]).wait()
-
-
-PLAN = "t0 w2 t1 w3 f0 t2 f1 o0 t3 f2 o1 f3 o2 o3"
 
 
 def per_device(groups, boxes_axis, coupling, inverse, tiles, near_block, neighbour, source_slot):
@@ -310,10 +308,12 @@
     lists = request_tables(neighbour, source_slot, device_now, boxes_axis * groups)
     half = jnp.bfloat16
     split = (box_count, groups, chunks, 2 * rows)
-    hbm = pl.BlockSpec(memory_space=pltpu.HBM)
+    hbm = pl.BlockSpec(memory_space=pl.ANY)
+    big = (coupling.reshape(split + (red,)), coupling, inverse, tiles.reshape(total, red, skel), near_block.reshape(split + (width,)))
+    big = [pltpu.with_memory_space_constraint(array, pltpu.HBM) for array in big]
     moved = pl.pallas_call(
         functools.partial(kernel, groups, boxes_axis, chunks, slots),
-        out_shape=jax.ShapeDtypeStruct((chunks, 2, groups, box_count, rows, width), half),
+        out_shape=pltpu.VMEM((chunks, 2, groups, box_count, rows, width), half),
         in_specs=[pl.BlockSpec(memory_space=pltpu.VMEM), hbm, hbm, hbm, hbm, hbm],
         out_specs=pl.BlockSpec(memory_space=pl.ANY),
         scratch_shapes=[
@@ -345,16 +345,12 @@
         + [pltpu.VMEM((2 * FAR + 1, chunk_rows, skel), half)] * chunks
         + [pltpu.VMEM((2 * groups, box_count, rows, width), half)] * chunks,
         compiler_params=pltpu.CompilerParams(
-            collective_id=0, has_side_effects=True, vmem_limit_bytes=46 * 2**20
+            collective_id=0, has_side_effects=True, vmem_limit_bytes=48 * 2**20
         ),
         cost_estimate=pl.CostEstimate(flops=9 * 10**9, bytes_accessed=24 * 10**6, transcendentals=0),
     )(
         lists,
-        coupling.reshape(split + (red,)),
-        coupling,
-        inverse,
-        tiles.reshape(total, red, skel),
-        near_block.reshape(split + (width,)),
+        *big,
     )
     return moved.reshape(-1, rows, width)
 

time: 128 us -> 124 us (0.969)
  local copies, waits for them, and re-layouts: 3.35 us -> 1.95 us
    pallas_call x1, Pallas kernels: 122 us -> 121 us  [per_device(): pl.pallas_call(functools.partial(kernel, groups, boxes_axis, chunks, slot...]
    unnamed x3 -> x1, local copies, waits for them, and re-layouts: 3.24 us -> 1.84 us
where the time goes in v3:
time: 124 us
  Pallas kernels  121 us (98%)
  local copies, waits for them, and re-layouts  1.95 us (2%)
    pallas_call x1, Pallas kernels, per_device(): pl.pallas_call(functools.partial(kernel, groups, boxes_axis, chunks, slot...  121 us

profile of v3, /device:TPU:0, one launch (start us, length us, event | category | flops | bytes accessed | tf_op | source)
XLA Modules:
  0.0 123.8 jit_solution(16432348018629556422)
XLA Ops:
  0.0 0.7 multiply_add_fusion
  0.7 0.1 copy.7
  0.8 0.1 select_reduce_fusion.2
  1.0 0.1 multiply_reduce_fusion
  1.1 0.1 select_reduce_fusion.1
  1.3 120.6 %shard_map.64 = bf16[4,2,4,4,8,1792]{5,4,3,2,1,0:T(8,128)(2,1)S(1)} custom-call(s32[3,8,128]{2,1,0:T(8,128)S(1)} %pad.9.lists, bf16[4,4,4,16,768]{4,3,2,1,0:T(8,128)(2,1)} %bitcast.32, bf16[4,256,768]{2,1,0:T(8,128)(2,1)} %coupling.1, bf16[4,768,768]{2,1,0:T(8,128)(2,1)} %inverse.1, bf16[24,768,256]{2,1,0:T(8,128)(2,1)} %bitcast.30, ...), custom_call_target="tpu_custom_call" | custom-call | flops 8999999488 | bytes 24000000 | tf_op jit(solution)/shard_map/pallas_call | solution.py:314
  121.9 1.8 %copy.9 = bf16[128,8,1792]{2,1,0:T(8,128)(2,1)} copy(bf16[128,8,1792]{2,1,0:T(8,128)(2,1)S(1)} %bitcast.29) | data formatting | bytes 7340032
  (16 shorter events, 0.1 us)

commit v4 on v3

--- a/solution.py
+++ b/solution.py
@@ -12,42 +12,11 @@
 MESH = pl.DeviceIdType.MESH
 
 
-def request_tables(neighbour, source_slot, device_now, device_count):
-    box_count, slot_count = neighbour.shape
-    total = box_count * slot_count
-    order = jnp.arange(total, dtype=jnp.int32)
-    spot = (jnp.arange(box_count)[:, None] * slot_count + jnp.arange(slot_count)[None, :]).astype(jnp.int32)
-    picks = (spot[None] == order[:, None, None]).astype(jnp.int32)
-    flat = jnp.sum(picks * (neighbour * slot_count + source_slot)[None], axis=(1, 2))
-    owner = flat // total
-    place = flat - owner * total
-    asked = jnp.stack(
-        [
-            owner == (device_now + 1) % device_count,
-            owner == (device_now + device_count - 1) % device_count,
-        ]
-    )
-    before = (order[None, :] < order[:, None]).astype(jnp.int32)
-    rank = jnp.sum(before[None] * asked[:, None, :].astype(jnp.int32), axis=2)
-    lanes = jnp.arange(128, dtype=jnp.int32)
-    onehot = jnp.logical_and(
-        jnp.logical_and(rank[:, None, :] == lanes[None, :, None], lanes[None, :, None] < FAR), asked[:, None, :]
-    ).astype(jnp.int32)
-    tile_list = jnp.sum(onehot * place[None, None, :], axis=2)
-    box_list = jnp.sum(onehot * (order // slot_count)[None, None, :], axis=2)
-    here = jnp.logical_not(jnp.logical_or(asked[0], asked[1]))
-    local_tile = jnp.where(here, place, total)
-    result_at = jnp.where(asked[0], rank[0], jnp.where(asked[1], FAR + rank[1], 2 * FAR))
-    own = jnp.pad(jnp.stack([local_tile, result_at]), ((0, 0), (0, 128 - total)))
-    rows = jnp.stack([jnp.stack([tile_list[0], box_list[0]]), jnp.stack([tile_list[1], box_list[1]]), own])
-    return jnp.pad(rows, ((0, 0), (0, 6), (0, 0)))
-
-
 def kernel(
     groups, boxes_axis, chunks, slots,
-    lists, split_coupling, coupling, inverse, tiles, split_near,
+    neighbour, source_slot, split_coupling, coupling, inverse, tiles, split_near,
     out,
-    cp, inv, full_c, tile, base, own_w, stage, list_in, list_s,
+    cp, inv, full_c, tile, base, own_w, stage, list_out, list_in, list_s, asked_s, place_s, near_s, slot_s,
     load_sem, c_sem, near_sem, list_send, list_recv, w_send, w_recv, r_send, r_recv,
     st_send, st_recv, out_send, out_recv, *buffers,
 ):
@@ -107,12 +76,16 @@
 
     load_tiles = pltpu.make_async_copy(tiles, tile.at[pl.ds(0, total)], load_sem.at[box_count])
     load_full = pltpu.make_async_copy(coupling, full_c, load_sem.at[box_count + 1])
-    load_own = pltpu.make_async_copy(lists.at[2], list_s.at[2], load_sem.at[box_count + 2])
+    load_own = [
+        pltpu.make_async_copy(neighbour, near_s, load_sem.at[box_count + 2]),
+        pltpu.make_async_copy(source_slot, slot_s, load_sem.at[box_count + 4]),
+    ]
     load_full.start()
     load_tiles.start()
     for q, dx in pieces:
         load_near(q, dx).start()
-    load_own.start()
+    for copy in load_own:
+        copy.start()
     tile[total] = jnp.zeros_like(tile[total])
     for q in range(chunks):
         res[q][2 * FAR] = jnp.zeros_like(res[q][2 * FAR])
@@ -129,11 +102,15 @@
             ).start()
 
     def send_w_all(q):
-        def one(a, carry):
-            send_w(q, a)
-            return carry
-
-        lax.fori_loop(0, box_count, one, 0)
+        for d in range(2):
+            pltpu.make_async_remote_copy(
+                src_ref=own_w.at[q],
+                dst_ref=wr[q].at[1 - d],
+                send_sem=w_send.at[q, d],
+                recv_sem=w_recv.at[q, 1 - d],
+                device_id=beside[d],
+                device_id_type=MESH,
+            ).start()
 
     for q, dx in pieces:
         load_c(q, dx).wait()
@@ -157,9 +134,40 @@
         return carry
 
     lax.fori_loop(0, box_count, weights_sent, 0)
+    for copy in load_own:
+        copy.wait()
+    taken = [0, 0]
+    for a in range(box_count):
+        for j in range(slots):
+            i = a * slots + j
+            owner = near_s[a, j] // box_count
+            place = (near_s[a, j] - owner * box_count) * slots + slot_s[a, j]
+            asked = [owner == after, owner == behind]
+            list_s[2, 0, i] = jnp.where(jnp.logical_or(asked[0], asked[1]), total, place)
+            list_s[2, 1, i] = jnp.where(asked[0], taken[0], jnp.where(asked[1], FAR + taken[1], 2 * FAR))
+            place_s[i] = place
+            for d in range(2):
+                asked_s[d, i] = jnp.where(asked[d], taken[d], -1)
+                taken[d] = taken[d] + jnp.where(asked[d], 1, 0)
+
+    def request(k, carry):
+        for d in range(2):
+            found_tile, found_box = 0, 0
+            for i in range(total):
+                match = asked_s[d, i] == k
+                found_tile = found_tile + jnp.where(match, place_s[i], 0)
+                found_box = found_box + jnp.where(match, i // slots, 0)
+            list_s[d, 0, k] = found_tile
+            list_s[d, 1, k] = found_box
+        return carry
+
+    lax.fori_loop(0, FAR, request, 0)
+    to_vectors = pltpu.make_async_copy(list_s.at[pl.ds(0, 2)], list_out, load_sem.at[box_count + 3])
+    to_vectors.start()
+    to_vectors.wait()
     list_copies = [
         pltpu.make_async_remote_copy(
-            src_ref=lists.at[d],
+            src_ref=list_out.at[d],
             dst_ref=list_in.at[1 - d],
             send_sem=list_send.at[d],
             recv_sem=list_recv.at[1 - d],
@@ -176,7 +184,6 @@
     load_tiles.wait()
     for q, dx in pieces:
         load_near(q, dx).wait()
-    load_own.wait()
 
     def local_terms(a, carry):
         w = own_w[:, a].reshape(skel, red)
@@ -186,7 +193,7 @@
         base[:, a, :, cols] = (near - own).astype(jnp.bfloat16).reshape(chunks, chunk_rows, skel)
         for j in range(slots):
             cols = pl.ds((j + 1) * skel, skel)
-            pair = jnp.dot(w, tile[list_s[2, 0, a * slots + j]], preferred_element_type=jnp.float32)
+            pair = jnp.dot(w, tile[jnp.clip(list_s[2, 0, a * slots + j], 0, total)], preferred_element_type=jnp.float32)
             near = base[:, a, :, cols].reshape(skel, skel).astype(jnp.float32)
             base[:, a, :, cols] = (near - pair).astype(jnp.bfloat16).reshape(chunks, chunk_rows, skel)
         return carry
@@ -196,7 +203,7 @@
 
     for copy in list_copies:
         copy.wait()
-    to_scalars = pltpu.make_async_copy(list_in, list_s.at[pl.ds(0, 2)], load_sem.at[box_count + 3])
+    to_scalars = pltpu.make_async_copy(list_in, list_s.at[pl.ds(0, 2)], load_sem.at[box_count + 2])
     to_scalars.start()
     to_scalars.wait()
 
@@ -208,9 +215,9 @@
             for d in range(2):
                 for i in range(GROUP):
                     k = n * GROUP + i
-                    pair = jnp.dot(
-                        wr[q][d, list_s[d, 1, k]], tile[list_s[d, 0, k]], preferred_element_type=jnp.float32
-                    )
+                    asked_box = jnp.clip(list_s[d, 1, k], 0, box_count - 1)
+                    asked_tile = jnp.clip(list_s[d, 0, k], 0, total)
+                    pair = jnp.dot(wr[q][d, asked_box], tile[asked_tile], preferred_element_type=jnp.float32)
                     rs[q][d, k] = pair.astype(jnp.bfloat16)
                 pltpu.make_async_remote_copy(
                     src_ref=rs[q].at[d, pl.ds(n * GROUP, GROUP)],
@@ -233,7 +240,8 @@
             ob[q][:, a, :, pl.ds(0, skel)] = base[q, a, :, pl.ds(0, skel)].reshape(dests, 8, skel)
             for j in range(slots):
                 cols = pl.ds((j + 1) * skel, skel)
-                value = base[q, a, :, cols].astype(jnp.float32) - res[q][list_s[2, 1, a * slots + j]].astype(jnp.float32)
+                arrived = res[q][jnp.clip(list_s[2, 1, a * slots + j], 0, 2 * FAR)]
+                value = base[q, a, :, cols].astype(jnp.float32) - arrived.astype(jnp.float32)
                 ob[q][:, a, :, cols] = value.reshape(dests, 8, skel).astype(jnp.bfloat16)
             return carry
 
@@ -304,17 +312,15 @@
     rows = skel // boxes_axis
     chunks = boxes_axis // groups // 2
     chunk_rows = skel // chunks
-    device_now = lax.axis_index(("box", "grp"))
-    lists = request_tables(neighbour, source_slot, device_now, boxes_axis * groups)
     half = jnp.bfloat16
     split = (box_count, groups, chunks, 2 * rows)
     hbm = pl.BlockSpec(memory_space=pl.ANY)
-    big = (coupling.reshape(split + (red,)), coupling, inverse, tiles.reshape(total, red, skel), near_block.reshape(split + (width,)))
+    big = (neighbour, source_slot, coupling.reshape(split + (red,)), coupling, inverse, tiles.reshape(total, red, skel), near_block.reshape(split + (width,)))
     big = [pltpu.with_memory_space_constraint(array, pltpu.HBM) for array in big]
     moved = pl.pallas_call(
         functools.partial(kernel, groups, boxes_axis, chunks, slots),
         out_shape=pltpu.VMEM((chunks, 2, groups, box_count, rows, width), half),
-        in_specs=[pl.BlockSpec(memory_space=pltpu.VMEM), hbm, hbm, hbm, hbm, hbm],
+        in_specs=[hbm] * 7,
         out_specs=pl.BlockSpec(memory_space=pl.ANY),
         scratch_shapes=[
             pltpu.VMEM((box_count, skel, red), half),
@@ -324,9 +330,14 @@
             pltpu.VMEM((chunks, box_count, chunk_rows, width), half),
             pltpu.VMEM((chunks, box_count, chunk_rows, red), half),
             pltpu.VMEM((groups, chunks, 2, box_count, rows, width), half),
-            pltpu.VMEM((2,) + lists.shape[1:], jnp.int32),
-            pltpu.SMEM(lists.shape, jnp.int32),
-            pltpu.SemaphoreType.DMA((box_count + 4,)),
+            pltpu.VMEM((2, 8, 128), jnp.int32),
+            pltpu.VMEM((2, 8, 128), jnp.int32),
+            pltpu.SMEM((3, 8, 128), jnp.int32),
+            pltpu.SMEM((2, total), jnp.int32),
+            pltpu.SMEM((total,), jnp.int32),
+            pltpu.SMEM(neighbour.shape, jnp.int32),
+            pltpu.SMEM(neighbour.shape, jnp.int32),
+            pltpu.SemaphoreType.DMA((box_count + 5,)),
             pltpu.SemaphoreType.DMA((chunks * groups,)),
             pltpu.SemaphoreType.DMA((chunks * groups,)),
             pltpu.SemaphoreType.DMA((2,)),
@@ -349,7 +360,6 @@
         ),
         cost_estimate=pl.CostEstimate(flops=9 * 10**9, bytes_accessed=24 * 10**6, transcendentals=0),
     )(
-        lists,
         *big,
     )
     return moved.reshape(-1, rows, width)

time: 124 us -> 123 us (level)
  no operation moved by 1% of the time
where the time goes in v4:
time: 123 us; the launch traced here: 122 us
  Pallas kernels  121 us (98%)
  local copies, waits for them, and re-layouts  1.84 us (1%)
    pallas_call x1, Pallas kernels, per_device(): pl.pallas_call(functools.partial(kernel, groups, boxes_axis, chunks, slot...  121 us

profile of v4, /device:TPU:0, one launch (start us, length us, event | category | flops | bytes accessed | tf_op | source)
XLA Modules:
  0.0 122.4 jit_solution(16725609670193097210)
XLA Ops:
  0.0 120.5 %shard_map.64 = bf16[4,2,4,4,8,1792]{5,4,3,2,1,0:T(8,128)(2,1)S(1)} custom-call(s32[4,6]{1,0:T(4,128)} %neighbour.1, s32[4,6]{1,0:T(4,128)} %source_slot.1, bf16[4,4,4,16,768]{4,3,2,1,0:T(8,128)(2,1)} %bitcast.7, bf16[4,256,768]{2,1,0:T(8,128)(2,1)} %coupling.1, bf16[4,768,768]{2,1,0:T(8,128)(2,1)} %inverse.1, bf16[24,768,256]{2,1,0:T(8,128)(2,1)} %bitcast.5, ...), custom_call_target="tpu_custom_call" | custom-call | flops 8999999488 | bytes 24000000 | tf_op jit(solution)/shard_map/pallas_call | solution.py:320
  120.5 1.8 %copy.8 = bf16[128,8,1792]{2,1,0:T(8,128)(2,1)} copy(bf16[128,8,1792]{2,1,0:T(8,128)(2,1)S(1)} %bitcast.4) | data formatting | bytes 7340032

commit v5 on v4

--- a/solution.py
+++ b/solution.py
@@ -112,13 +112,19 @@
                 device_id_type=MESH,
             ).start()
 
-    for q, dx in pieces:
-        load_c(q, dx).wait()
+    for dx in range(groups):
+        load_c(0, dx).wait()
 
     def weights(a, carry):
         load_inv(a).wait()
-        product = jnp.dot(cp[a], inv[a], preferred_element_type=jnp.float32)
-        own_w[:, a] = product.astype(jnp.bfloat16).reshape(chunks, chunk_rows, red)
+        product = jnp.dot(cp[a, pl.ds(0, chunk_rows)], inv[a], preferred_element_type=jnp.float32)
+        own_w[0, a] = product.astype(jnp.bfloat16)
+        return carry
+
+    def later_weights(a, carry):
+        rows = pl.ds(chunk_rows, skel - chunk_rows)
+        product = jnp.dot(cp[a, rows], inv[a], preferred_element_type=jnp.float32)
+        own_w[pl.ds(1, chunks - 1), a] = product.astype(jnp.bfloat16).reshape(chunks - 1, chunk_rows, red)
         return carry
 
     lax.fori_loop(0, 1, weights, 0)
@@ -134,6 +140,9 @@
         return carry
 
     lax.fori_loop(0, box_count, weights_sent, 0)
+    for q, dx in pieces[groups:]:
+        load_c(q, dx).wait()
+    lax.fori_loop(0, box_count, later_weights, 0)
     for copy in load_own:
         copy.wait()
     taken = [0, 0]

time: 123 us -> 123 us (level)
  no operation moved by 1% of the time
where the time goes in v5:
time: 123 us
  Pallas kernels  121 us (98%)
  local copies, waits for them, and re-layouts  1.84 us (1%)
    pallas_call x1, Pallas kernels, per_device(): pl.pallas_call(functools.partial(kernel, groups, boxes_axis, chunks, slot...  121 us

profile of v5, /device:TPU:0, one launch (start us, length us, event | category | flops | bytes accessed | tf_op | source)
XLA Modules:
  0.0 122.6 jit_solution(5523773510868836371)
XLA Ops:
  0.0 120.8 %shard_map.64 = bf16[4,2,4,4,8,1792]{5,4,3,2,1,0:T(8,128)(2,1)S(1)} custom-call(s32[4,6]{1,0:T(4,128)} %neighbour.1, s32[4,6]{1,0:T(4,128)} %source_slot.1, bf16[4,4,4,16,768]{4,3,2,1,0:T(8,128)(2,1)} %bitcast.7, bf16[4,256,768]{2,1,0:T(8,128)(2,1)} %coupling.1, bf16[4,768,768]{2,1,0:T(8,128)(2,1)} %inverse.1, bf16[24,768,256]{2,1,0:T(8,128)(2,1)} %bitcast.5, ...), custom_call_target="tpu_custom_call" | custom-call | flops 8999999488 | bytes 24000000 | tf_op jit(solution)/shard_map/pallas_call | solution.py:329
  120.8 1.8 %copy.8 = bf16[128,8,1792]{2,1,0:T(8,128)(2,1)} copy(bf16[128,8,1792]{2,1,0:T(8,128)(2,1)S(1)} %bitcast.4) | data formatting | bytes 7340032
